TPU v7x, 256 devices: a whole 4x4x8 slice. The times are simulated.
256 devices in a mesh: grp: 8 (over x, core), row: 32 (over y, z).
Axes of the slice: x: 4, y: 4, z: 8, core: 2. Of those that a mesh axis runs over, the one named last changes fastest.
Arguments:
- features: bfloat16 [8192, 8192], P('row', 'grp'), may hold values from -0.0625 to 0.0625
- residual: float32 [8192, 576], P('row'), may hold values from -6 to 6
- precond: float32 [8192, 1024], P('grp'), as said below
Outputs:
- coefs: float32 [8192, 576], P('grp')
- section_resid: float32 [8, 8192, 576], P('grp', 'row')
Inputs may be any that keep to these rules, and one draw needn't show every extreme that they name: Each 1024 x 1024 block of precond is symmetric and positive definite.
All inputs are finite; a program needn't handle non-finite values.
Results may differ from a plain program's by a relative error of at most 0.009.
Values may be sent and summed in bfloat16 or wider, within the bound.
A program may use at most 64 MiB of HBM per device.

v0:
```python
import jax
import jax.numpy as jnp
from jax import lax
from jax.sharding import PartitionSpec as P


def from_behind(block, axis, distance):
    devices = range(lax.axis_size(axis))
    route = [(i - distance, i) for i in devices if i - distance in devices]
    return lax.ppermute(block, axis, route)


def chain_sweep(features, residual, precond):
    section_index = lax.axis_index("grp")
    section_count = lax.axis_size("grp")
    row_count, target_width = residual.shape
    block_width = features.shape[1]
    panel_count = 3
    panel_width = target_width // panel_count
    step_count = section_count + panel_count - 1

    def correlate(rounded):
        correlation = lax.dot_general(
            features, rounded, (((0,), (0,)), ((), ())), preferred_element_type=jnp.float32
        )
        correlation = lax.psum(correlation, "row")
        share = block_width // lax.axis_size("row")
        first = lax.axis_index("row") * share
        own_map = lax.dynamic_slice_in_dim(precond, first, share, 0)
        own_rows = jnp.dot(own_map, correlation, precision=lax.Precision.HIGHEST)
        return lax.all_gather(own_rows, "row", axis=0, tiled=True)

    def turn(turn_index, loop_state):
        current, coef_table, resid_table = loop_state
        position = turn_index - section_index
        inside = jnp.logical_and(position >= 0, position < panel_count)
        panel_slot = jnp.clip(position, 0, panel_count - 1) * panel_width
        fresh_panel = lax.dynamic_slice_in_dim(residual, panel_slot, panel_width, 1)
        current = jnp.where(section_index == 0, fresh_panel, current)
        rounded = current.astype(jnp.bfloat16)
        coefficient = correlate(rounded)
        updated = current - jnp.dot(
            features, coefficient.astype(jnp.bfloat16), preferred_element_type=jnp.float32
        )
        old_coef = lax.dynamic_slice_in_dim(coef_table, panel_slot, panel_width, 1)
        coef_table = lax.dynamic_update_slice_in_dim(
            coef_table, jnp.where(inside, coefficient, old_coef), panel_slot, 1
        )
        old_resid = lax.dynamic_slice_in_dim(resid_table, panel_slot, panel_width, 2)
        resid_table = lax.dynamic_update_slice_in_dim(
            resid_table, jnp.where(inside, updated[None], old_resid), panel_slot, 2
        )
        passed = from_behind(updated, "grp", 1)
        return (passed, coef_table, resid_table)

    start_state = (
        jnp.zeros((row_count, panel_width), jnp.float32),
        jnp.zeros((block_width, target_width), jnp.float32),
        jnp.zeros((1, row_count, target_width), jnp.float32),
    )
    final_state = lax.fori_loop(0, step_count, turn, start_state)
    return (final_state[1], final_state[2])


def local(features, residual, precond):
    return chain_sweep(features, residual, precond)


def solution(mesh):
    placed = (P("row", "grp"), P("row", None), P("grp", None))
    return jax.shard_map(
        local,
        mesh=mesh,
        in_specs=placed,
        out_specs=(P("grp", None), P("grp", "row", None)),
        check_vma=False,
    )
```

profile of v0, /device:TPU:1, one launch (start us, length us, event | category | flops | bytes accessed | tf_op | source)
XLA Modules:
  0.0 2120.8 jit_solution(15154932183782905294)
XLA Ops:
  9.8 2104.2 %while.18 = (s32[]{:T(128)}, f32[256,192]{0,1:T(8,128)S(1)}, f32[1024,576]{0,1:T(8,128)}, f32[1,256,576]{1,2,0:T(8,128)}, pred[]{:T(512)}, /*index=5*/s32[]{:T(1...) while((s32[]{:T(128)}, f32[256,192]{0,1:T(8,128)S(1)}, ...), condition=%wide.region_2.3_spmd, body=%wide.region_0.2_spmd.sunk | while | flops 277610496 | bytes 19809716 | solution.py:61
  9.8 2.1 convolution_bitcast_fusion.3
  13.4 148.3 %all-reduce.2.cloned.1.call-done = f32[1024,192]{0,1:T(8,128)} async-done(((f32[1024,192]{0,1:T(8,128)}), f32[1024,192]{0,1:T(8,128)}) %all-reduce.2.cloned.1.call-update) | async-done | bytes 786448 | tf_op jit(solution)/shard_map/while/body/eval_jaxpr/psum | solution.py:26
  163.7 36.9 %all_gather.9 = f32[1024,192]{1,0:T(8,128)S(1)} all-gather(f32[32,192]{1,0:T(8,128)S(1)} %fusion.23), channel_id=1, replica_groups=mesh['grp'=8,'row'=32] {'row'}, dimensions={0}, use_global_device_ids=true | all-gather | bytes 811008 | tf_op jit(solution)/shard_map/while/body/eval_jaxpr/all_gather | solution.py:31
  202.7 20.0 collective-permute-start
  228.9 142.8 %all-reduce.2.cloned.1.call-done = f32[1024,192]{0,1:T(8,128)} async-done(((f32[1024,192]{0,1:T(8,128)}), f32[1024,192]{0,1:T(8,128)}) %all-reduce.2.cloned.1.call-update) | async-done | bytes 786448 | tf_op jit(solution)/shard_map/while/body/eval_jaxpr/psum | solution.py:26
  373.7 36.9 %all_gather.9 = f32[1024,192]{1,0:T(8,128)S(1)} all-gather(f32[32,192]{1,0:T(8,128)S(1)} %fusion.23), channel_id=1, replica_groups=mesh['grp'=8,'row'=32] {'row'}, dimensions={0}, use_global_device_ids=true | all-gather | bytes 811008 | tf_op jit(solution)/shard_map/while/body/eval_jaxpr/all_gather | solution.py:31
  412.7 20.0 collective-permute-start
  438.9 142.8 %all-reduce.2.cloned.1.call-done = f32[1024,192]{0,1:T(8,128)} async-done(((f32[1024,192]{0,1:T(8,128)}), f32[1024,192]{0,1:T(8,128)}) %all-reduce.2.cloned.1.call-update) | async-done | bytes 786448 | tf_op jit(solution)/shard_map/while/body/eval_jaxpr/psum | solution.py:26
  583.7 36.9 %all_gather.9 = f32[1024,192]{1,0:T(8,128)S(1)} all-gather(f32[32,192]{1,0:T(8,128)S(1)} %fusion.23), channel_id=1, replica_groups=mesh['grp'=8,'row'=32] {'row'}, dimensions={0}, use_global_device_ids=true | all-gather | bytes 811008 | tf_op jit(solution)/shard_map/while/body/eval_jaxpr/all_gather | solution.py:31
  622.7 20.0 collective-permute-start
  648.9 142.4 %all-reduce.2.cloned.1.call-done = f32[1024,192]{0,1:T(8,128)} async-done(((f32[1024,192]{0,1:T(8,128)}), f32[1024,192]{0,1:T(8,128)}) %all-reduce.2.cloned.1.call-update) | async-done | bytes 786448 | tf_op jit(solution)/shard_map/while/body/eval_jaxpr/psum | solution.py:26
  793.4 36.9 %all_gather.9 = f32[1024,192]{1,0:T(8,128)S(1)} all-gather(f32[32,192]{1,0:T(8,128)S(1)} %fusion.23), channel_id=1, replica_groups=mesh['grp'=8,'row'=32] {'row'}, dimensions={0}, use_global_device_ids=true | all-gather | bytes 811008 | tf_op jit(solution)/shard_map/while/body/eval_jaxpr/all_gather | solution.py:31
  832.4 20.0 collective-permute-start
  858.6 142.4 %all-reduce.2.cloned.1.call-done = f32[1024,192]{0,1:T(8,128)} async-done(((f32[1024,192]{0,1:T(8,128)}), f32[1024,192]{0,1:T(8,128)}) %all-reduce.2.cloned.1.call-update) | async-done | bytes 786448 | tf_op jit(solution)/shard_map/while/body/eval_jaxpr/psum | solution.py:26
  1003.1 36.9 %all_gather.9 = f32[1024,192]{1,0:T(8,128)S(1)} all-gather(f32[32,192]{1,0:T(8,128)S(1)} %fusion.23), channel_id=1, replica_groups=mesh['grp'=8,'row'=32] {'row'}, dimensions={0}, use_global_device_ids=true | all-gather | bytes 811008 | tf_op jit(solution)/shard_map/while/body/eval_jaxpr/all_gather | solution.py:31
  1042.1 20.0 collective-permute-start
  1068.3 142.5 %all-reduce.2.cloned.1.call-done = f32[1024,192]{0,1:T(8,128)} async-done(((f32[1024,192]{0,1:T(8,128)}), f32[1024,192]{0,1:T(8,128)}) %all-reduce.2.cloned.1.call-update) | async-done | bytes 786448 | tf_op jit(solution)/shard_map/while/body/eval_jaxpr/psum | solution.py:26
  1212.8 36.9 %all_gather.9 = f32[1024,192]{1,0:T(8,128)S(1)} all-gather(f32[32,192]{1,0:T(8,128)S(1)} %fusion.23), channel_id=1, replica_groups=mesh['grp'=8,'row'=32] {'row'}, dimensions={0}, use_global_device_ids=true | all-gather | bytes 811008 | tf_op jit(solution)/shard_map/while/body/eval_jaxpr/all_gather | solution.py:31
  1251.8 20.0 collective-permute-start
  1278.0 142.8 %all-reduce.2.cloned.1.call-done = f32[1024,192]{0,1:T(8,128)} async-done(((f32[1024,192]{0,1:T(8,128)}), f32[1024,192]{0,1:T(8,128)}) %all-reduce.2.cloned.1.call-update) | async-done | bytes 786448 | tf_op jit(solution)/shard_map/while/body/eval_jaxpr/psum | solution.py:26
  1422.8 36.9 %all_gather.9 = f32[1024,192]{1,0:T(8,128)S(1)} all-gather(f32[32,192]{1,0:T(8,128)S(1)} %fusion.23), channel_id=1, replica_groups=mesh['grp'=8,'row'=32] {'row'}, dimensions={0}, use_global_device_ids=true | all-gather | bytes 811008 | tf_op jit(solution)/shard_map/while/body/eval_jaxpr/all_gather | solution.py:31
  1461.8 20.0 collective-permute-start
  1488.0 142.7 %all-reduce.2.cloned.1.call-done = f32[1024,192]{0,1:T(8,128)} async-done(((f32[1024,192]{0,1:T(8,128)}), f32[1024,192]{0,1:T(8,128)}) %all-reduce.2.cloned.1.call-update) | async-done | bytes 786448 | tf_op jit(solution)/shard_map/while/body/eval_jaxpr/psum | solution.py:26
  1632.8 36.9 %all_gather.9 = f32[1024,192]{1,0:T(8,128)S(1)} all-gather(f32[32,192]{1,0:T(8,128)S(1)} %fusion.23), channel_id=1, replica_groups=mesh['grp'=8,'row'=32] {'row'}, dimensions={0}, use_global_device_ids=true | all-gather | bytes 811008 | tf_op jit(solution)/shard_map/while/body/eval_jaxpr/all_gather | solution.py:31
  1671.7 20.0 collective-permute-start
  1698.0 142.8 %all-reduce.2.cloned.1.call-done = f32[1024,192]{0,1:T(8,128)} async-done(((f32[1024,192]{0,1:T(8,128)}), f32[1024,192]{0,1:T(8,128)}) %all-reduce.2.cloned.1.call-update) | async-done | bytes 786448 | tf_op jit(solution)/shard_map/while/body/eval_jaxpr/psum | solution.py:26
  1842.8 36.9 %all_gather.9 = f32[1024,192]{1,0:T(8,128)S(1)} all-gather(f32[32,192]{1,0:T(8,128)S(1)} %fusion.23), channel_id=1, replica_groups=mesh['grp'=8,'row'=32] {'row'}, dimensions={0}, use_global_device_ids=true | all-gather | bytes 811008 | tf_op jit(solution)/shard_map/while/body/eval_jaxpr/all_gather | solution.py:31
  1881.8 20.0 collective-permute-start
  1908.0 142.4 %all-reduce.2.cloned.1.call-done = f32[1024,192]{0,1:T(8,128)} async-done(((f32[1024,192]{0,1:T(8,128)}), f32[1024,192]{0,1:T(8,128)}) %all-reduce.2.cloned.1.call-update) | async-done | bytes 786448 | tf_op jit(solution)/shard_map/while/body/eval_jaxpr/psum | solution.py:26
  2052.5 36.9 %all_gather.9 = f32[1024,192]{1,0:T(8,128)S(1)} all-gather(f32[32,192]{1,0:T(8,128)S(1)} %fusion.23), channel_id=1, replica_groups=mesh['grp'=8,'row'=32] {'row'}, dimensions={0}, use_global_device_ids=true | all-gather | bytes 811008 | tf_op jit(solution)/shard_map/while/body/eval_jaxpr/all_gather | solution.py:31
  2091.4 20.0 collective-permute-start
  (114 shorter events, 103.3 us)
Async XLA Ops:
  7.2 2.6 copy-start
  9.8 151.9 %all-reduce.2.cloned.1.call-start = ((), (), s32[]{:S(2)}) async-start(), calls=%async_computation | async-start | bytes 1572864 | tf_op jit(solution)/shard_map/while/body/eval_jaxpr/psum | solution.py:26
  202.7 22.6 %collective-permute-start = (f32[256,192]{0,1:T(8,128)S(1)}, f32[256,192]{0,1:T(8,128)S(1)}, u32[]{:S(2)}, u32[]{:S(2)}) collective-permute-start(f32[256,192]{0,1:T(8,128)S(1)} %get-tuple-element.260), channel_id=1, source_target_pairs={{0,32},{32,64},{64,96},{96,128},{128,160},{160,192},{192,224},{1,3... | collective-permute-start | bytes 589832 | tf_op jit(solution)/shard_map/while/body/eval_jaxpr/ppermute | solution.py:10
  225.3 146.4 %all-reduce.2.cloned.1.call-start = ((), (), s32[]{:S(2)}) async-start(), calls=%async_computation | async-start | bytes 1572864 | tf_op jit(solution)/shard_map/while/body/eval_jaxpr/psum | solution.py:26
  412.7 22.6 %collective-permute-start = (f32[256,192]{0,1:T(8,128)S(1)}, f32[256,192]{0,1:T(8,128)S(1)}, u32[]{:S(2)}, u32[]{:S(2)}) collective-permute-start(f32[256,192]{0,1:T(8,128)S(1)} %get-tuple-element.260), channel_id=1, source_target_pairs={{0,32},{32,64},{64,96},{96,128},{128,160},{160,192},{192,224},{1,3... | collective-permute-start | bytes 589832 | tf_op jit(solution)/shard_map/while/body/eval_jaxpr/ppermute | solution.py:10
  435.3 146.4 %all-reduce.2.cloned.1.call-start = ((), (), s32[]{:S(2)}) async-start(), calls=%async_computation | async-start | bytes 1572864 | tf_op jit(solution)/shard_map/while/body/eval_jaxpr/psum | solution.py:26
  622.7 22.6 %collective-permute-start = (f32[256,192]{0,1:T(8,128)S(1)}, f32[256,192]{0,1:T(8,128)S(1)}, u32[]{:S(2)}, u32[]{:S(2)}) collective-permute-start(f32[256,192]{0,1:T(8,128)S(1)} %get-tuple-element.260), channel_id=1, source_target_pairs={{0,32},{32,64},{64,96},{96,128},{128,160},{160,192},{192,224},{1,3... | collective-permute-start | bytes 589832 | tf_op jit(solution)/shard_map/while/body/eval_jaxpr/ppermute | solution.py:10
  645.3 146.1 %all-reduce.2.cloned.1.call-start = ((), (), s32[]{:S(2)}) async-start(), calls=%async_computation | async-start | bytes 1572864 | tf_op jit(solution)/shard_map/while/body/eval_jaxpr/psum | solution.py:26
  832.4 22.6 %collective-permute-start = (f32[256,192]{0,1:T(8,128)S(1)}, f32[256,192]{0,1:T(8,128)S(1)}, u32[]{:S(2)}, u32[]{:S(2)}) collective-permute-start(f32[256,192]{0,1:T(8,128)S(1)} %get-tuple-element.260), channel_id=1, source_target_pairs={{0,32},{32,64},{64,96},{96,128},{128,160},{160,192},{192,224},{1,3... | collective-permute-start | bytes 589832 | tf_op jit(solution)/shard_map/while/body/eval_jaxpr/ppermute | solution.py:10
  855.0 146.1 %all-reduce.2.cloned.1.call-start = ((), (), s32[]{:S(2)}) async-start(), calls=%async_computation | async-start | bytes 1572864 | tf_op jit(solution)/shard_map/while/body/eval_jaxpr/psum | solution.py:26
  1042.1 22.6 %collective-permute-start = (f32[256,192]{0,1:T(8,128)S(1)}, f32[256,192]{0,1:T(8,128)S(1)}, u32[]{:S(2)}, u32[]{:S(2)}) collective-permute-start(f32[256,192]{0,1:T(8,128)S(1)} %get-tuple-element.260), channel_id=1, source_target_pairs={{0,32},{32,64},{64,96},{96,128},{128,160},{160,192},{192,224},{1,3... | collective-permute-start | bytes 589832 | tf_op jit(solution)/shard_map/while/body/eval_jaxpr/ppermute | solution.py:10
  1064.7 146.1 %all-reduce.2.cloned.1.call-start = ((), (), s32[]{:S(2)}) async-start(), calls=%async_computation | async-start | bytes 1572864 | tf_op jit(solution)/shard_map/while/body/eval_jaxpr/psum | solution.py:26
  1251.8 22.6 %collective-permute-start = (f32[256,192]{0,1:T(8,128)S(1)}, f32[256,192]{0,1:T(8,128)S(1)}, u32[]{:S(2)}, u32[]{:S(2)}) collective-permute-start(f32[256,192]{0,1:T(8,128)S(1)} %get-tuple-element.260), channel_id=1, source_target_pairs={{0,32},{32,64},{64,96},{96,128},{128,160},{160,192},{192,224},{1,3... | collective-permute-start | bytes 589832 | tf_op jit(solution)/shard_map/while/body/eval_jaxpr/ppermute | solution.py:10
  1274.4 146.4 %all-reduce.2.cloned.1.call-start = ((), (), s32[]{:S(2)}) async-start(), calls=%async_computation | async-start | bytes 1572864 | tf_op jit(solution)/shard_map/while/body/eval_jaxpr/psum | solution.py:26
  1461.8 22.6 %collective-permute-start = (f32[256,192]{0,1:T(8,128)S(1)}, f32[256,192]{0,1:T(8,128)S(1)}, u32[]{:S(2)}, u32[]{:S(2)}) collective-permute-start(f32[256,192]{0,1:T(8,128)S(1)} %get-tuple-element.260), channel_id=1, source_target_pairs={{0,32},{32,64},{64,96},{96,128},{128,160},{160,192},{192,224},{1,3... | collective-permute-start | bytes 589832 | tf_op jit(solution)/shard_map/while/body/eval_jaxpr/ppermute | solution.py:10
  1484.4 146.4 %all-reduce.2.cloned.1.call-start = ((), (), s32[]{:S(2)}) async-start(), calls=%async_computation | async-start | bytes 1572864 | tf_op jit(solution)/shard_map/while/body/eval_jaxpr/psum | solution.py:26
  1671.7 22.6 %collective-permute-start = (f32[256,192]{0,1:T(8,128)S(1)}, f32[256,192]{0,1:T(8,128)S(1)}, u32[]{:S(2)}, u32[]{:S(2)}) collective-permute-start(f32[256,192]{0,1:T(8,128)S(1)} %get-tuple-element.260), channel_id=1, source_target_pairs={{0,32},{32,64},{64,96},{96,128},{128,160},{160,192},{192,224},{1,3... | collective-permute-start | bytes 589832 | tf_op jit(solution)/shard_map/while/body/eval_jaxpr/ppermute | solution.py:10
  1694.3 146.4 %all-reduce.2.cloned.1.call-start = ((), (), s32[]{:S(2)}) async-start(), calls=%async_computation | async-start | bytes 1572864 | tf_op jit(solution)/shard_map/while/body/eval_jaxpr/psum | solution.py:26
  1881.8 22.6 %collective-permute-start = (f32[256,192]{0,1:T(8,128)S(1)}, f32[256,192]{0,1:T(8,128)S(1)}, u32[]{:S(2)}, u32[]{:S(2)}) collective-permute-start(f32[256,192]{0,1:T(8,128)S(1)} %get-tuple-element.260), channel_id=1, source_target_pairs={{0,32},{32,64},{64,96},{96,128},{128,160},{160,192},{192,224},{1,3... | collective-permute-start | bytes 589832 | tf_op jit(solution)/shard_map/while/body/eval_jaxpr/ppermute | solution.py:10
  1904.3 146.1 %all-reduce.2.cloned.1.call-start = ((), (), s32[]{:S(2)}) async-start(), calls=%async_computation | async-start | bytes 1572864 | tf_op jit(solution)/shard_map/while/body/eval_jaxpr/psum | solution.py:26
  2091.4 22.6 %collective-permute-start = (f32[256,192]{0,1:T(8,128)S(1)}, f32[256,192]{0,1:T(8,128)S(1)}, u32[]{:S(2)}, u32[]{:S(2)}) collective-permute-start(f32[256,192]{0,1:T(8,128)S(1)} %get-tuple-element.260), channel_id=1, source_target_pairs={{0,32},{32,64},{64,96},{96,128},{128,160},{160,192},{192,224},{1,3... | collective-permute-start | bytes 589832 | tf_op jit(solution)/shard_map/while/body/eval_jaxpr/ppermute | solution.py:10
Sparse Core Ops, SparseCore 0:
  13.9 147.6 all-reduce.1
  229.4 142.1 all-reduce.1
  439.4 142.2 all-reduce.1
  649.1 142.1 all-reduce.1
  858.8 142.1 all-reduce.1
  1068.5 142.2 all-reduce.1
  1278.5 142.1 all-reduce.1
  1488.5 142.1 all-reduce.1
  1698.5 142.2 all-reduce.1
  1908.2 142.1 all-reduce.1
where the time goes:
time: 2120 us
  waiting for transfers between devices  1440 us (68%)
  blocking collectives  369 us (17%)
  starting transfers between devices  200 us (9%)
  matrix products  61.7 us (3%)
  local copies, waits for them, and re-layouts  30.3 us (1%)
    psum x10, waiting for transfers between devices, correlate(): correlation = lax.psum(correlation, 'row')  1430 us
    all_gather x10, blocking collectives, correlate(): return lax.all_gather(own_rows, 'row', axis=0, tiled=True)  369 us
    ppermute x10, starting transfers between devices, from_behind(): return lax.ppermute(block, axis, route)  200 us
  transfers between devices with their start and end apart: 20, of which 20 were waited for; matrix products, arithmetic and copies ran while one was open for 1% of the time, Pallas kernels for 0%

commit v1 on v0

--- a/solution.py
+++ b/solution.py
@@ -23,7 +23,7 @@
         correlation = lax.dot_general(
             features, rounded, (((0,), (0,)), ((), ())), preferred_element_type=jnp.float32
         )
-        correlation = lax.psum(correlation, "row")
+        correlation = jnp.sum(lax.all_gather(correlation, "row"), axis=0)
         share = block_width // lax.axis_size("row")
         first = lax.axis_index("row") * share
         own_map = lax.dynamic_slice_in_dim(precond, first, share, 0)

time: 2120 us -> 2740 us (1.29)
  waiting for transfers between devices: 1440 us -> 1830 us
  local copies, waits for them, and re-layouts: 30.3 us -> 251 us
  other arithmetic: 1.39 us -> 58.4 us
  starting transfers between devices: 200 us -> 163 us
    all_gather x0 -> x10, waiting for transfers between devices: none -> 1820 us  [correlate(): correlation = jnp.sum(lax.all_gather(correlation, 'row'), axis=0)]
    psum x10 -> x0, waiting for transfers between devices: 1430 us -> none  [correlate(): correlation = lax.psum(correlation, 'row')]
    while x0 -> x10, local copies, waits for them, and re-layouts: none -> 221 us
    reduce_sum x0 -> x10, other arithmetic: none -> 57 us  [correlate(): correlation = jnp.sum(lax.all_gather(correlation, 'row'), axis=0)]
    ppermute x10, starting transfers between devices: 200 us -> 163 us  [from_behind(): return lax.ppermute(block, axis, route)]
where the time goes in v1:
time: 2740 us
  waiting for transfers between devices  1830 us (67%)
  blocking collectives  361 us (13%)
  local copies, waits for them, and re-layouts  251 us (9%)
  starting transfers between devices  163 us (6%)
  matrix products  59 us (2%)
  other arithmetic  58.4 us (2%)
    all_gather x10, waiting for transfers between devices, correlate(): correlation = jnp.sum(lax.all_gather(correlation, 'row'), axis=0)  1820 us
    all_gather x10, blocking collectives, correlate(): return lax.all_gather(own_rows, 'row', axis=0, tiled=True)  361 us
    while x10, local copies, waits for them, and re-layouts  221 us
    ppermute x10, starting transfers between devices, from_behind(): return lax.ppermute(block, axis, route)  163 us
    reduce_sum x10, other arithmetic, correlate(): correlation = jnp.sum(lax.all_gather(correlation, 'row'), axis=0)  57 us
  transfers between devices with their start and end apart: 20, of which 20 were waited for; matrix products, arithmetic and copies ran while one was open for 1% of the time, Pallas kernels for 0%

profile of v1, /device:TPU:1, one launch (start us, length us, event | category | flops | bytes accessed | tf_op | source)
XLA Modules:
  0.0 2741.7 jit_solution(17878483497337027546)
XLA Ops:
  9.8 2725.1 %while.18 = (s32[]{:T(128)}, f32[256,192]{0,1:T(8,128)S(1)}, f32[1024,576]{0,1:T(8,128)}, f32[1,256,576]{1,2,0:T(8,128)}, pred[]{:T(512)}, /*index=5*/s32[]{:T(1...) while((s32[]{:T(128)}, f32[256,192]{0,1:T(8,128)S(1)}, ...), condition=%wide.region_2.3_spmd, body=%wide.region_0.2_spmd.sunk | while | flops 283508736 | bytes 169231808 | solution.py:61
  13.5 186.9 %all-gather.5.cloned.1.call-done = f32[32768,192]{0,1:T(8,128)} async-done(((f32[1024,192]{0,1:T(8,128)}), f32[32768,192]{0,1:T(8,128)}) %all-gather.5.cloned.1.call-update) | async-done | bytes 25165840 | tf_op jit(solution)/shard_map/while/body/eval_jaxpr/all_gather | solution.py:26
  200.4 22.1 copy.14
  230.0 36.1 %all_gather.25 = f32[1024,192]{1,0:T(8,128)S(1)} all-gather(f32[32,192]{1,0:T(8,128)S(1)} %fusion.23), channel_id=1, replica_groups=mesh['grp'=8,'row'=32] {'row'}, dimensions={0}, use_global_device_ids=true | all-gather | bytes 811008 | tf_op jit(solution)/shard_map/while/body/eval_jaxpr/all_gather | solution.py:31
  290.8 181.8 %all-gather.5.cloned.1.call-done = f32[32768,192]{0,1:T(8,128)} async-done(((f32[1024,192]{0,1:T(8,128)}), f32[32768,192]{0,1:T(8,128)}) %all-gather.5.cloned.1.call-update) | async-done | bytes 25165840 | tf_op jit(solution)/shard_map/while/body/eval_jaxpr/all_gather | solution.py:26
  472.6 22.1 copy.14
  502.1 36.1 %all_gather.25 = f32[1024,192]{1,0:T(8,128)S(1)} all-gather(f32[32,192]{1,0:T(8,128)S(1)} %fusion.23), channel_id=1, replica_groups=mesh['grp'=8,'row'=32] {'row'}, dimensions={0}, use_global_device_ids=true | all-gather | bytes 811008 | tf_op jit(solution)/shard_map/while/body/eval_jaxpr/all_gather | solution.py:31
  562.9 181.8 %all-gather.5.cloned.1.call-done = f32[32768,192]{0,1:T(8,128)} async-done(((f32[1024,192]{0,1:T(8,128)}), f32[32768,192]{0,1:T(8,128)}) %all-gather.5.cloned.1.call-update) | async-done | bytes 25165840 | tf_op jit(solution)/shard_map/while/body/eval_jaxpr/all_gather | solution.py:26
  744.7 22.1 copy.14
  774.3 36.1 %all_gather.25 = f32[1024,192]{1,0:T(8,128)S(1)} all-gather(f32[32,192]{1,0:T(8,128)S(1)} %fusion.23), channel_id=1, replica_groups=mesh['grp'=8,'row'=32] {'row'}, dimensions={0}, use_global_device_ids=true | all-gather | bytes 811008 | tf_op jit(solution)/shard_map/while/body/eval_jaxpr/all_gather | solution.py:31
  835.0 181.5 %all-gather.5.cloned.1.call-done = f32[32768,192]{0,1:T(8,128)} async-done(((f32[1024,192]{0,1:T(8,128)}), f32[32768,192]{0,1:T(8,128)}) %all-gather.5.cloned.1.call-update) | async-done | bytes 25165840 | tf_op jit(solution)/shard_map/while/body/eval_jaxpr/all_gather | solution.py:26
  1016.5 22.1 copy.14
  1046.1 36.1 %all_gather.25 = f32[1024,192]{1,0:T(8,128)S(1)} all-gather(f32[32,192]{1,0:T(8,128)S(1)} %fusion.23), channel_id=1, replica_groups=mesh['grp'=8,'row'=32] {'row'}, dimensions={0}, use_global_device_ids=true | all-gather | bytes 811008 | tf_op jit(solution)/shard_map/while/body/eval_jaxpr/all_gather | solution.py:31
  1106.8 181.5 %all-gather.5.cloned.1.call-done = f32[32768,192]{0,1:T(8,128)} async-done(((f32[1024,192]{0,1:T(8,128)}), f32[32768,192]{0,1:T(8,128)}) %all-gather.5.cloned.1.call-update) | async-done | bytes 25165840 | tf_op jit(solution)/shard_map/while/body/eval_jaxpr/all_gather | solution.py:26
  1288.3 22.1 copy.14
  1317.9 36.1 %all_gather.25 = f32[1024,192]{1,0:T(8,128)S(1)} all-gather(f32[32,192]{1,0:T(8,128)S(1)} %fusion.23), channel_id=1, replica_groups=mesh['grp'=8,'row'=32] {'row'}, dimensions={0}, use_global_device_ids=true | all-gather | bytes 811008 | tf_op jit(solution)/shard_map/while/body/eval_jaxpr/all_gather | solution.py:31
  1378.6 181.5 %all-gather.5.cloned.1.call-done = f32[32768,192]{0,1:T(8,128)} async-done(((f32[1024,192]{0,1:T(8,128)}), f32[32768,192]{0,1:T(8,128)}) %all-gather.5.cloned.1.call-update) | async-done | bytes 25165840 | tf_op jit(solution)/shard_map/while/body/eval_jaxpr/all_gather | solution.py:26
  1560.1 22.1 copy.14
  1589.7 36.1 %all_gather.25 = f32[1024,192]{1,0:T(8,128)S(1)} all-gather(f32[32,192]{1,0:T(8,128)S(1)} %fusion.23), channel_id=1, replica_groups=mesh['grp'=8,'row'=32] {'row'}, dimensions={0}, use_global_device_ids=true | all-gather | bytes 811008 | tf_op jit(solution)/shard_map/while/body/eval_jaxpr/all_gather | solution.py:31
  1650.4 181.8 %all-gather.5.cloned.1.call-done = f32[32768,192]{0,1:T(8,128)} async-done(((f32[1024,192]{0,1:T(8,128)}), f32[32768,192]{0,1:T(8,128)}) %all-gather.5.cloned.1.call-update) | async-done | bytes 25165840 | tf_op jit(solution)/shard_map/while/body/eval_jaxpr/all_gather | solution.py:26
  1832.2 22.1 copy.14
  1861.8 36.1 %all_gather.25 = f32[1024,192]{1,0:T(8,128)S(1)} all-gather(f32[32,192]{1,0:T(8,128)S(1)} %fusion.23), channel_id=1, replica_groups=mesh['grp'=8,'row'=32] {'row'}, dimensions={0}, use_global_device_ids=true | all-gather | bytes 811008 | tf_op jit(solution)/shard_map/while/body/eval_jaxpr/all_gather | solution.py:31
  1922.5 181.8 %all-gather.5.cloned.1.call-done = f32[32768,192]{0,1:T(8,128)} async-done(((f32[1024,192]{0,1:T(8,128)}), f32[32768,192]{0,1:T(8,128)}) %all-gather.5.cloned.1.call-update) | async-done | bytes 25165840 | tf_op jit(solution)/shard_map/while/body/eval_jaxpr/all_gather | solution.py:26
  2104.4 22.1 copy.14
  2133.9 36.1 %all_gather.25 = f32[1024,192]{1,0:T(8,128)S(1)} all-gather(f32[32,192]{1,0:T(8,128)S(1)} %fusion.23), channel_id=1, replica_groups=mesh['grp'=8,'row'=32] {'row'}, dimensions={0}, use_global_device_ids=true | all-gather | bytes 811008 | tf_op jit(solution)/shard_map/while/body/eval_jaxpr/all_gather | solution.py:31
  2172.1 16.3 collective-permute-start
  2194.7 181.8 %all-gather.5.cloned.1.call-done = f32[32768,192]{0,1:T(8,128)} async-done(((f32[1024,192]{0,1:T(8,128)}), f32[32768,192]{0,1:T(8,128)}) %all-gather.5.cloned.1.call-update) | async-done | bytes 25165840 | tf_op jit(solution)/shard_map/while/body/eval_jaxpr/all_gather | solution.py:26
  2376.5 22.1 copy.14
  2406.0 36.1 %all_gather.25 = f32[1024,192]{1,0:T(8,128)S(1)} all-gather(f32[32,192]{1,0:T(8,128)S(1)} %fusion.23), channel_id=1, replica_groups=mesh['grp'=8,'row'=32] {'row'}, dimensions={0}, use_global_device_ids=true | all-gather | bytes 811008 | tf_op jit(solution)/shard_map/while/body/eval_jaxpr/all_gather | solution.py:31
  2466.8 181.5 %all-gather.5.cloned.1.call-done = f32[32768,192]{0,1:T(8,128)} async-done(((f32[1024,192]{0,1:T(8,128)}), f32[32768,192]{0,1:T(8,128)}) %all-gather.5.cloned.1.call-update) | async-done | bytes 25165840 | tf_op jit(solution)/shard_map/while/body/eval_jaxpr/all_gather | solution.py:26
  2648.3 22.1 copy.14
  2677.8 36.1 %all_gather.25 = f32[1024,192]{1,0:T(8,128)S(1)} all-gather(f32[32,192]{1,0:T(8,128)S(1)} %fusion.23), channel_id=1, replica_groups=mesh['grp'=8,'row'=32] {'row'}, dimensions={0}, use_global_device_ids=true | all-gather | bytes 811008 | tf_op jit(solution)/shard_map/while/body/eval_jaxpr/all_gather | solution.py:31
  (134 shorter events, 306.4 us)
Async XLA Ops:
  7.2 2.6 copy-start
  9.8 190.7 %all-gather.5.cloned.1.call-start = ((), (), s32[]{:S(2)}) async-start(), calls=%async_computation | async-start | bytes 25952256 | tf_op jit(solution)/shard_map/while/body/eval_jaxpr/all_gather | solution.py:26
  268.2 18.9 collective-permute-start
  287.1 185.5 %all-gather.5.cloned.1.call-start = ((), (), s32[]{:S(2)}) async-start(), calls=%async_computation | async-start | bytes 25952256 | tf_op jit(solution)/shard_map/while/body/eval_jaxpr/all_gather | solution.py:26
  540.3 18.9 collective-permute-start
  559.2 185.5 %all-gather.5.cloned.1.call-start = ((), (), s32[]{:S(2)}) async-start(), calls=%async_computation | async-start | bytes 25952256 | tf_op jit(solution)/shard_map/while/body/eval_jaxpr/all_gather | solution.py:26
  812.4 18.9 collective-permute-start
  831.3 185.2 %all-gather.5.cloned.1.call-start = ((), (), s32[]{:S(2)}) async-start(), calls=%async_computation | async-start | bytes 25952256 | tf_op jit(solution)/shard_map/while/body/eval_jaxpr/all_gather | solution.py:26
  1084.2 18.9 collective-permute-start
  1103.1 185.2 %all-gather.5.cloned.1.call-start = ((), (), s32[]{:S(2)}) async-start(), calls=%async_computation | async-start | bytes 25952256 | tf_op jit(solution)/shard_map/while/body/eval_jaxpr/all_gather | solution.py:26
  1356.0 18.9 collective-permute-start
  1374.9 185.2 %all-gather.5.cloned.1.call-start = ((), (), s32[]{:S(2)}) async-start(), calls=%async_computation | async-start | bytes 25952256 | tf_op jit(solution)/shard_map/while/body/eval_jaxpr/all_gather | solution.py:26
  1627.8 18.9 collective-permute-start
  1646.7 185.5 %all-gather.5.cloned.1.call-start = ((), (), s32[]{:S(2)}) async-start(), calls=%async_computation | async-start | bytes 25952256 | tf_op jit(solution)/shard_map/while/body/eval_jaxpr/all_gather | solution.py:26
  1899.9 18.9 collective-permute-start
  1918.8 185.5 %all-gather.5.cloned.1.call-start = ((), (), s32[]{:S(2)}) async-start(), calls=%async_computation | async-start | bytes 25952256 | tf_op jit(solution)/shard_map/while/body/eval_jaxpr/all_gather | solution.py:26
  2172.1 18.9 collective-permute-start
  2191.0 185.5 %all-gather.5.cloned.1.call-start = ((), (), s32[]{:S(2)}) async-start(), calls=%async_computation | async-start | bytes 25952256 | tf_op jit(solution)/shard_map/while/body/eval_jaxpr/all_gather | solution.py:26
  2444.2 18.9 collective-permute-start
  2463.1 185.2 %all-gather.5.cloned.1.call-start = ((), (), s32[]{:S(2)}) async-start(), calls=%async_computation | async-start | bytes 25952256 | tf_op jit(solution)/shard_map/while/body/eval_jaxpr/all_gather | solution.py:26
  2716.0 18.9 collective-permute-start
Sparse Core Ops, SparseCore 0:
  13.2 187.2 all-gather.4
  290.5 182.0 all-gather.4
  562.6 182.0 all-gather.4
  834.4 182.0 all-gather.4
  1106.2 182.0 all-gather.4
  1378.0 182.0 all-gather.4
  1650.1 182.0 all-gather.4
  1922.2 182.0 all-gather.4
  2194.4 182.0 all-gather.4
  2466.2 182.0 all-gather.4
